TPU v7x, 128 devices: a whole 4x4x4 slice. The times are simulated.
128 devices in a mesh: dp: 32 (over y_lo, z, x), seq: 4 (over y_hi, core).
Axes of the slice: x: 4, y: 4 (y_hi: 2, y_lo: 2; y = y_hi * 2 + y_lo), z: 4, core: 2. Of those that a mesh axis runs over, the one named last changes fastest.
Arguments:
- inputs: bfloat16 [32, 580, 1024], P('dp', 'seq'), may hold values from -6 to 6
- token_mask: int32 [32, 580], P('dp', 'seq'), may hold values from 0 to 1, as said below
- first_gain: bfloat16 [1, 1024], P(None, ('dp', 'seq')), may hold values from 0.5 to 1.5
- first_shift: bfloat16 [1, 1024], P(None, ('dp', 'seq')), may hold values from -3 to 3
- query_key_value_weight: bfloat16 [1, 1024, 3072], P(None, ('dp', 'seq')), may hold values from -0.1875 to 0.1875
- query_value_bias: bfloat16 [1, 2048], P(None, ('dp', 'seq')), may hold values from -3 to 3
- output_weight: bfloat16 [1, 1024, 1024], P(None, ('dp', 'seq')), may hold values from -0.75 to 0.75
- output_bias: bfloat16 [1, 1024], P(None, ('dp', 'seq')), may hold values from -3 to 3
- second_gain: bfloat16 [1, 1024], P(None, ('dp', 'seq')), may hold values from 0.5 to 1.5
- second_shift: bfloat16 [1, 1024], P(None, ('dp', 'seq')), may hold values from -3 to 3
- up_weight: bfloat16 [1, 1024, 4096], P(None, ('dp', 'seq')), may hold values from -0.1875 to 0.1875
- up_bias: bfloat16 [1, 4096], P(None, ('dp', 'seq')), may hold values from -3 to 3
- down_weight: bfloat16 [1, 4096, 1024], P(None, ('dp', 'seq')), may hold values from -0.09375 to 0.09375
- down_bias: bfloat16 [1, 1024], P(None, ('dp', 'seq')), may hold values from -3 to 3
- cotangent: bfloat16 [32, 580, 1024], P('dp', 'seq'), may hold values from -6 to 6
Outputs:
- block_output: bfloat16 [32, 580, 1024], P('dp', 'seq')
- input_gradient: float32 [32, 580, 1024], P('dp', 'seq')
- first_gain_gradient: float32 [1, 1024], P(None, ('dp', 'seq'))
- first_shift_gradient: float32 [1, 1024], P(None, ('dp', 'seq'))
- query_key_value_weight_gradient: float32 [1, 1024, 3072], P(None, ('dp', 'seq'))
- query_value_bias_gradient: float32 [1, 2048], P(None, ('dp', 'seq'))
- output_weight_gradient: float32 [1, 1024, 1024], P(None, ('dp', 'seq'))
- output_bias_gradient: float32 [1, 1024], P(None, ('dp', 'seq'))
- second_gain_gradient: float32 [1, 1024], P(None, ('dp', 'seq'))
- second_shift_gradient: float32 [1, 1024], P(None, ('dp', 'seq'))
- up_weight_gradient: float32 [1, 1024, 4096], P(None, ('dp', 'seq'))
- up_bias_gradient: float32 [1, 4096], P(None, ('dp', 'seq'))
- down_weight_gradient: float32 [1, 4096, 1024], P(None, ('dp', 'seq'))
- down_bias_gradient: float32 [1, 1024], P(None, ('dp', 'seq'))
Inputs may be any that keep to these rules, and one draw needn't show every extreme that they name: In every image the positions with token_mask 1 are the first ones, more than 435 of them; image 0 has exactly its last min(3, 144) positions at 0.
All inputs are finite; a program needn't handle non-finite values.
Results may differ from a plain program's by a relative error of at most 0.017.
Values may be sent and summed in bfloat16 or wider, within the bound.
No kernel may reach another device: no remote copies, remote signals or barrier semaphores. Data moves between devices by JAX's collectives and lax.ppermute only.
A program may use at most 192 MiB of HBM per device.

v0:
```python
import jax
import jax.numpy as jnp
from jax import lax
from jax.sharding import PartitionSpec as P

HEADS = 16
HEAD_DIM = 64


def layer_norm(values_in, gain_vector, offset_vector):
    average = jnp.mean(values_in, axis=-1, keepdims=True)
    centred = values_in - average
    variance = jnp.mean(centred * centred, axis=-1, keepdims=True)
    return centred * lax.rsqrt(variance + 1e-06) * gain_vector + offset_vector


def gelu_exact(values_in):
    return jax.nn.gelu(values_in, approximate=False)


def attention_scores(query_block, key_block, keep_all):
    images, local_tokens, model_width = query_block.shape
    query_heads = query_block.reshape(images, local_tokens, HEADS, HEAD_DIM)
    key_heads = key_block.reshape(images, key_block.shape[1], HEADS, HEAD_DIM)
    raw_scores = jnp.einsum(
        "bqhd,bkhd->bhqk", query_heads, key_heads, preferred_element_type=jnp.float32
    ) * HEAD_DIM ** (-0.5)
    return jnp.where(keep_all[:, None, None, :] > 0, raw_scores, -1e30)


def forward_layer(hidden, key_keep, weights):
    (
        attend_gain,
        attend_shift,
        inward_matrix,
        inward_bias,
        outward_matrix,
        outward_bias,
        feed_gain,
        feed_shift,
        expand_matrix,
        expand_bias,
        reduce_matrix,
        reduce_bias,
    ) = weights
    images, local_tokens, model_width = hidden.shape
    row_count = images * local_tokens
    flat_input = hidden.reshape(row_count, model_width)
    normed_first = layer_norm(flat_input, attend_gain, attend_shift).astype(jnp.bfloat16)
    projected = jnp.dot(normed_first, inward_matrix, preferred_element_type=jnp.float32)
    queries = (
        (projected[:, :model_width] + inward_bias[:model_width])
        .astype(jnp.bfloat16)
        .reshape(images, local_tokens, model_width)
    )
    keys_here = (
        projected[:, model_width : 2 * model_width]
        .astype(jnp.bfloat16)
        .reshape(images, local_tokens, model_width)
    )
    values_here = (
        (projected[:, 2 * model_width :] + inward_bias[model_width:])
        .astype(jnp.bfloat16)
        .reshape(images, local_tokens, model_width)
    )
    keys_all, values_all, keep_all = (
        lax.all_gather(keys_here, "seq", axis=1, tiled=True),
        lax.all_gather(values_here, "seq", axis=1, tiled=True),
        lax.all_gather(key_keep, "seq", axis=1, tiled=True),
    )
    scores = attention_scores(queries, keys_all, keep_all)
    row_peak = jnp.max(scores, axis=-1, keepdims=True)
    log_total = row_peak + jnp.log(jnp.sum(jnp.exp(scores - row_peak), axis=-1, keepdims=True))
    probs_low = jnp.exp(scores - log_total).astype(jnp.bfloat16)
    value_heads = values_all.reshape(images, values_all.shape[1], HEADS, HEAD_DIM)
    mixed = jnp.einsum(
        "bhqk,bkhd->bqhd", probs_low, value_heads, preferred_element_type=jnp.float32
    )
    mixed = mixed.reshape(row_count, model_width).astype(jnp.bfloat16)
    residual = (
        flat_input
        + jnp.dot(mixed, outward_matrix, preferred_element_type=jnp.float32)
        + outward_bias
    )
    normed_second = layer_norm(residual, feed_gain, feed_shift).astype(jnp.bfloat16)
    expanded = (
        jnp.dot(normed_second, expand_matrix, preferred_element_type=jnp.float32) + expand_bias
    )
    activated = gelu_exact(expanded).astype(jnp.bfloat16)
    output_rows = (
        residual
        + jnp.dot(activated, reduce_matrix, preferred_element_type=jnp.float32)
        + reduce_bias
    )
    saved = (
        flat_input,
        key_keep,
        queries,
        keys_here,
        values_here,
        keys_all,
        values_all,
        keep_all,
        log_total,
        mixed,
        residual,
        expanded,
    )
    return (output_rows.reshape(images, local_tokens, model_width), saved)


def backward_layer(grad_out, saved, weights):
    (
        attend_gain,
        attend_shift,
        inward_matrix,
        inward_bias,
        outward_matrix,
        outward_bias,
        feed_gain,
        feed_shift,
        expand_matrix,
        expand_bias,
        reduce_matrix,
        reduce_bias,
    ) = weights
    (
        flat_input,
        key_keep,
        queries,
        keys_here,
        values_here,
        keys_all,
        values_all,
        keep_all,
        log_total,
        mixed,
        residual,
        expanded,
    ) = saved
    images, local_tokens, model_width = queries.shape
    row_count = images * local_tokens
    grad_reduce = grad_out.astype(jnp.bfloat16)
    gelu_value, gelu_pull = jax.vjp(gelu_exact, expanded)
    activated = gelu_value.astype(jnp.bfloat16)
    reduce_matrix_gradient = jnp.einsum(
        "rf,rd->fd", activated, grad_reduce, preferred_element_type=jnp.float32
    )
    reduce_bias_gradient = jnp.sum(grad_reduce, axis=0, dtype=jnp.float32)
    grad_activated = jnp.einsum(
        "rd,fd->rf", grad_reduce, reduce_matrix, preferred_element_type=jnp.float32
    )
    grad_expanded = gelu_pull(grad_activated)[0].astype(jnp.bfloat16)
    feed_normed, feed_pull = jax.vjp(
        layer_norm, residual, feed_gain.astype(jnp.float32), feed_shift.astype(jnp.float32)
    )
    expand_matrix_gradient = jnp.einsum(
        "rd,rf->df",
        feed_normed.astype(jnp.bfloat16),
        grad_expanded,
        preferred_element_type=jnp.float32,
    )
    expand_bias_gradient = jnp.sum(grad_expanded, axis=0, dtype=jnp.float32)
    grad_feed_normed = jnp.einsum(
        "rf,df->rd", grad_expanded, expand_matrix, preferred_element_type=jnp.float32
    )
    grad_through_feed, feed_gain_gradient, feed_shift_gradient = feed_pull(grad_feed_normed)
    grad_residual = grad_out + grad_through_feed
    grad_attend = grad_residual.astype(jnp.bfloat16)
    outward_matrix_gradient = jnp.einsum(
        "rd,re->de", mixed, grad_attend, preferred_element_type=jnp.float32
    )
    outward_bias_gradient = jnp.sum(grad_attend, axis=0, dtype=jnp.float32)
    grad_mixed = jnp.einsum(
        "re,de->rd", grad_attend, outward_matrix, preferred_element_type=jnp.float32
    ).astype(jnp.bfloat16)
    scores = attention_scores(queries, keys_all, keep_all)
    probs = jnp.exp(scores - log_total)
    probs_low = probs.astype(jnp.bfloat16)
    key_count = keys_all.shape[1]
    grad_heads = grad_mixed.reshape(images, local_tokens, HEADS, HEAD_DIM)
    query_heads = queries.reshape(images, local_tokens, HEADS, HEAD_DIM)
    key_heads = keys_all.reshape(images, key_count, HEADS, HEAD_DIM)
    value_heads = values_all.reshape(images, key_count, HEADS, HEAD_DIM)
    grad_values_part = jnp.einsum(
        "bhqk,bqhd->bkhd", probs_low, grad_heads, preferred_element_type=jnp.float32
    )
    grad_probs = jnp.einsum(
        "bqhd,bkhd->bhqk", grad_heads, value_heads, preferred_element_type=jnp.float32
    )
    row_inner = jnp.sum(probs * grad_probs, axis=-1, keepdims=True)
    grad_scores = (probs * (grad_probs - row_inner)).astype(jnp.bfloat16)
    grad_queries = jnp.einsum(
        "bhqk,bkhd->bqhd", grad_scores, key_heads, preferred_element_type=jnp.float32
    ) * HEAD_DIM ** (-0.5)
    grad_queries = grad_queries.reshape(row_count, model_width).astype(jnp.bfloat16)
    grad_keys_part = jnp.einsum(
        "bhqk,bqhd->bkhd", grad_scores, query_heads, preferred_element_type=jnp.float32
    ) * HEAD_DIM ** (-0.5)
    grad_keys, grad_values = (
        lax.psum_scatter(
            grad_keys_part.reshape(images, key_count, model_width).astype(jnp.bfloat16),
            "seq",
            scatter_dimension=1,
            tiled=True,
        ).astype(jnp.float32),
        lax.psum_scatter(
            grad_values_part.reshape(images, key_count, model_width).astype(jnp.bfloat16),
            "seq",
            scatter_dimension=1,
            tiled=True,
        ).astype(jnp.float32),
    )
    grad_keys = grad_keys.reshape(row_count, model_width).astype(jnp.bfloat16)
    grad_values = grad_values.reshape(row_count, model_width).astype(jnp.bfloat16)
    grad_projected = jnp.concatenate([grad_queries, grad_keys, grad_values], axis=1)
    attend_normed, attend_pull = jax.vjp(
        layer_norm, flat_input, attend_gain.astype(jnp.float32), attend_shift.astype(jnp.float32)
    )
    inward_matrix_gradient = jnp.einsum(
        "rd,re->de",
        attend_normed.astype(jnp.bfloat16),
        grad_projected,
        preferred_element_type=jnp.float32,
    )
    inward_bias_gradient = jnp.concatenate(
        [
            jnp.sum(grad_queries, axis=0, dtype=jnp.float32),
            jnp.sum(grad_values, axis=0, dtype=jnp.float32),
        ]
    )
    grad_attend_normed = jnp.einsum(
        "re,de->rd", grad_projected, inward_matrix, preferred_element_type=jnp.float32
    )
    grad_through_attend, attend_gain_gradient, attend_shift_gradient = attend_pull(
        grad_attend_normed
    )
    grad_input = grad_residual + grad_through_attend
    gradients = (
        attend_gain_gradient,
        attend_shift_gradient,
        inward_matrix_gradient,
        inward_bias_gradient,
        outward_matrix_gradient,
        outward_bias_gradient,
        feed_gain_gradient,
        feed_shift_gradient,
        expand_matrix_gradient,
        expand_bias_gradient,
        reduce_matrix_gradient,
        reduce_bias_gradient,
    )
    return (grad_input, gradients)


def body(
    inputs,
    token_mask,
    first_gain,
    first_shift,
    query_key_value_weight,
    query_value_bias,
    output_weight,
    output_bias,
    second_gain,
    second_shift,
    up_weight,
    up_bias,
    down_weight,
    down_bias,
    cotangent,
):
    images, local_tokens, model_width = inputs.shape
    depth = first_gain.shape[0]
    key_keep = token_mask.astype(jnp.bfloat16)
    hidden = inputs.astype(jnp.float32)
    layer_index = 0
    fetched = (
        lax.all_gather(first_gain[layer_index], ("dp", "seq"), axis=0, tiled=True),
        lax.all_gather(first_shift[layer_index], ("dp", "seq"), axis=0, tiled=True),
        lax.all_gather(query_key_value_weight[layer_index], ("dp", "seq"), axis=0, tiled=True),
        lax.all_gather(query_value_bias[layer_index], ("dp", "seq"), axis=0, tiled=True),
        lax.all_gather(output_weight[layer_index], ("dp", "seq"), axis=0, tiled=True),
        lax.all_gather(output_bias[layer_index], ("dp", "seq"), axis=0, tiled=True),
        lax.all_gather(second_gain[layer_index], ("dp", "seq"), axis=0, tiled=True),
        lax.all_gather(second_shift[layer_index], ("dp", "seq"), axis=0, tiled=True),
        lax.all_gather(up_weight[layer_index], ("dp", "seq"), axis=0, tiled=True),
        lax.all_gather(up_bias[layer_index], ("dp", "seq"), axis=0, tiled=True),
        lax.all_gather(down_weight[layer_index], ("dp", "seq"), axis=0, tiled=True),
        lax.all_gather(down_bias[layer_index], ("dp", "seq"), axis=0, tiled=True),
    )
    hidden, saved = forward_layer(hidden, key_keep, fetched)
    saved_layers = [saved]
    fetched_layers = [fetched]
    block_output = hidden.astype(jnp.bfloat16)
    grad_hidden = cotangent.astype(jnp.float32).reshape(images * local_tokens, model_width)
    shard_gradients = []
    for layer_index in reversed(range(depth)):
        fetched = fetched_layers[layer_index]
        grad_hidden, gradients = backward_layer(grad_hidden, saved_layers[layer_index], fetched)
        (
            grad_gain_one,
            grad_shift_one,
            grad_inward,
            grad_inward_bias,
            grad_outward,
            grad_outward_bias,
            grad_gain_two,
            grad_shift_two,
            grad_expand,
            grad_expand_bias,
            grad_reduce,
            grad_reduce_bias,
        ) = gradients
        summed = (
            lax.psum_scatter(grad_gain_one, ("dp", "seq"), scatter_dimension=0, tiled=True),
            lax.psum_scatter(grad_shift_one, ("dp", "seq"), scatter_dimension=0, tiled=True),
            lax.psum_scatter(grad_inward, ("dp", "seq"), scatter_dimension=0, tiled=True),
            lax.psum_scatter(grad_inward_bias, ("dp", "seq"), scatter_dimension=0, tiled=True),
            lax.psum_scatter(grad_outward, ("dp", "seq"), scatter_dimension=0, tiled=True),
            lax.psum_scatter(grad_outward_bias, ("dp", "seq"), scatter_dimension=0, tiled=True),
            lax.psum_scatter(grad_gain_two, ("dp", "seq"), scatter_dimension=0, tiled=True),
            lax.psum_scatter(grad_shift_two, ("dp", "seq"), scatter_dimension=0, tiled=True),
            lax.psum_scatter(grad_expand, ("dp", "seq"), scatter_dimension=0, tiled=True),
            lax.psum_scatter(grad_expand_bias, ("dp", "seq"), scatter_dimension=0, tiled=True),
            lax.psum_scatter(grad_reduce, ("dp", "seq"), scatter_dimension=0, tiled=True),
            lax.psum_scatter(grad_reduce_bias, ("dp", "seq"), scatter_dimension=0, tiled=True),
        )
        shard_gradients.insert(0, summed)
    stacked = tuple(
        (
            jnp.stack([per_layer[member_index] for per_layer in shard_gradients])
            for member_index in range(12)
        )
    )
    input_gradient = grad_hidden.reshape(images, local_tokens, model_width)
    return (block_output, input_gradient) + stacked


def solution(mesh):
    return jax.shard_map(
        body,
        mesh=mesh,
        in_specs=(
            P("dp", "seq", None),
            P("dp", "seq"),
            P(None, ("dp", "seq")),
            P(None, ("dp", "seq")),
            P(None, ("dp", "seq"), None),
            P(None, ("dp", "seq")),
            P(None, ("dp", "seq"), None),
            P(None, ("dp", "seq")),
            P(None, ("dp", "seq")),
            P(None, ("dp", "seq")),
            P(None, ("dp", "seq"), None),
            P(None, ("dp", "seq")),
            P(None, ("dp", "seq"), None),
            P(None, ("dp", "seq")),
            P("dp", "seq", None),
        ),
        out_specs=(
            P("dp", "seq", None),
            P("dp", "seq", None),
            P(None, ("dp", "seq")),
            P(None, ("dp", "seq")),
            P(None, ("dp", "seq"), None),
            P(None, ("dp", "seq")),
            P(None, ("dp", "seq"), None),
            P(None, ("dp", "seq")),
            P(None, ("dp", "seq")),
            P(None, ("dp", "seq")),
            P(None, ("dp", "seq"), None),
            P(None, ("dp", "seq")),
            P(None, ("dp", "seq"), None),
            P(None, ("dp", "seq")),
        ),
        check_vma=False,
    )
```

profile of v0, /device:TPU:0, one launch (start us, length us, event | category | flops | bytes accessed | tf_op | source)
XLA Modules:
  0.0 3605.2 jit_solution(17541575675454655155)
XLA Ops:
  7.2 0.7 all-gather.23.cloned.1.call-update
  8.0 0.8 dynamic-update-slice.5
  8.8 0.8 dynamic-update-slice.6
  9.7 0.8 dynamic-update-slice.4
  10.5 0.8 dynamic-update-slice
  11.3 0.8 dynamic-update-slice.1
  12.2 0.8 dynamic-update-slice.8
  13.0 0.8 dynamic-update-slice.2
  13.8 0.8 dynamic-update-slice.7
  14.7 68.7 %all-reduce.20 = (bf16[1024]{0:T(1024)(128)(2,1)S(1)}, bf16[1024]{0:T(1024)(128)(2,1)S(1)}, bf16[2048]{0:T(1024)(128)(2,1)S(1)}, bf16[1024]{0:T(1024)(128)(2,1)S...) all-reduce(bf16[1024]{0:T(1024)(128)(2,1)S(1)} %dynamic-update-slic, ...), channel_id=3, replica_groups=mesh['dp'=32,'seq'=4] {'dp','seq'}, use_global_device_ids=true, to_apply=%add.1 | all-reduce | flops 12288 | bytes 49152
  83.3 1.1 convert_reduce_fusion.4
  84.5 1.2 fusion.62
  85.7 127.9 %all-gather.23.cloned.1.call-done = bf16[1,1024,3072]{2,1,0:T(8,128)(2,1)} async-done(((bf16[1,8,3072]{2,1,0:T(8,128)(2,1)}), bf16[1,1024,3072]{2,1,0:T(8,128)(2,1)}) %all-gather.23.cloned.1.call-update) | async-done | bytes 6291472 | tf_op jit(solution)/shard_map/all_gather | solution.py:281
  213.6 4.1 fusion.10
  217.8 0.8 fusion.68
  218.7 0.9 fusion.64
  223.0 8.3 all-reduce.3
  231.5 7.6 all-gather.33.cloned.1.call-done
  239.1 3.7 reshape.337
  242.7 3.9 copy.53
  246.6 16.0 all-gather.31.cloned.1.call-done
  262.6 3.7 reshape.336
  266.3 3.9 copy.52
  270.1 1.3 fusion.15
  271.5 1.8 exponential_reduce_fusion
  273.3 0.8 copy-done
  274.2 2.0 convolution_convert_fusion.1
  276.1 181.9 %all-gather.25.cloned.1.call-done = bf16[1,1024,1024]{2,1,0:T(8,128)(2,1)} async-done(((bf16[1,8,1024]{2,1,0:T(8,128)(2,1)}), bf16[1,1024,1024]{2,1,0:T(8,128)(2,1)}) %all-gather.25.cloned.1.call-update) | async-done | bytes 2097168 | tf_op jit(solution)/shard_map/all_gather | solution.py:283
  458.1 2.2 fusion.90
  460.5 200.7 %all-gather.27.cloned.1.call-done = bf16[1,1024,4096]{2,1,0:T(8,128)(2,1)} async-done(((bf16[1,8,4096]{2,1,0:T(8,128)(2,1)}), bf16[1,1024,4096]{2,1,0:T(8,128)(2,1)}) %all-gather.27.cloned.1.call-update) | async-done | bytes 8388624 | tf_op jit(solution)/shard_map/all_gather | solution.py:287
  661.3 10.5 multiply_convert_fusion.2
  671.8 192.7 %all-gather.29.cloned.1.call-done = bf16[1,4096,1024]{2,1,0:T(8,128)(2,1)} async-done(((bf16[1,32,1024]{2,1,0:T(8,128)(2,1)}), bf16[1,4096,1024]{2,1,0:T(8,128)(2,1)}) %all-gather.29.cloned.1.call-update) | async-done | bytes 8388624 | tf_op jit(solution)/shard_map/all_gather | solution.py:289
  864.5 11.0 convert_reduce_fusion
  875.5 3.1 multiply_reduce_fusion.1
  879.2 0.7 copy-done.10
  879.8 0.6 copy-done.9
  880.5 1.6 fusion.45
  882.0 1.2 copy.59
  883.2 5.7 convolution_convert_fusion
  889.0 2.5 multiply_reduce_fusion
  891.5 2.2 multiply_convert_fusion
  893.7 1.6 copy-done.1
  895.3 1.9 multiply_convert_fusion.1
  897.3 1.0 copy-done.21
  898.3 2.8 fusion.91
  902.0 1.0 copy-done.2
  903.0 3.5 convert_reduce_fusion.2
  906.4 57.0 %all-reduce.24.cloned.1.call-done = (bf16[1,580,1024]{1,2,0:T(8,128)(2,1)}, bf16[1,580,1024]{1,2,0:T(8,128)(2,1)}) async-done(((bf16[1,580,1024]{1,2,0:T(8,128)(2,1)}, bf16[1,580,1024]{1,2,0:T(8,128)(2,1)}), (bf16[1,580,1024]{1,2,0:T(8,128)(2,1)}, bf16[1,580,1024]{1,2,0:T(8,128)(2,1)})) %all-reduce.24.cloned.1.call-update) | async-done | bytes 2375696
  963.5 1.6 convert_reduce_fusion.1
  965.0 1.6 dynamic-slice_bitcast_fusion.1
  966.6 0.8 copy-done.25
  967.4 7.5 fusion.58
  975.1 1.0 copy-done.4
  976.5 8.3 fusion.85
  985.0 1.0 copy-done.7
  986.1 8.2 fusion.69
  994.4 5.7 fusion.48
  1000.1 5.2 fusion.86
  1006.1 1.4 copy.51
  1007.6 67.0 %all-reduce.19 = (f32[1024]{0:T(1024)S(1)}, f32[1024]{0:T(1024)S(1)}, f32[2048]{0:T(1024)S(1)}, f32[1024]{0:T(1024)S(1)}, f32[1024]{0:T(1024)S(1)}, /*index=5*/f...) all-reduce(f32[1024]{0:T(1024)S(1)} %get-tuple-element.58, ...), channel_id=18, replica_groups=mesh['dp'=32,'seq'=4] {'dp','seq'}, use_global_device_ids=true, to_apply=%region_14.15.clone | all-reduce | flops 12288 | bytes 98304
  1077.5 533.1 %reduce-scatter.9.cloned.1.call-done = f32[8,1024]{1,0:T(8,128)} async-done(((f32[1024,1024]{1,0:T(8,128)}), f32[8,1024]{1,0:T(8,128)}) %reduce-scatter.9.cloned.1.call-update) | async-done | bytes 32784 | tf_op jit(solution)/shard_map/reduce_scatter | solution.py:320
  1610.6 656.6 %reduce-scatter.7.cloned.1.call-done = f32[8,3072]{1,0:T(8,128)} async-done(((f32[1024,3072]{1,0:T(8,128)}), f32[8,3072]{1,0:T(8,128)}) %reduce-scatter.7.cloned.1.call-update) | async-done | bytes 98320 | tf_op jit(solution)/shard_map/reduce_scatter | solution.py:318
  2267.2 665.6 %reduce-scatter.11.cloned.1.call-done = f32[8,4096]{1,0:T(8,128)} async-done(((f32[1024,4096]{1,0:T(8,128)}), f32[8,4096]{1,0:T(8,128)}) %reduce-scatter.11.cloned.1.call-update) | async-done | bytes 131088 | tf_op jit(solution)/shard_map/reduce_scatter | solution.py:324
  2932.8 665.7 %reduce-scatter.13.cloned.1.call-done = f32[32,1024]{1,0:T(8,128)} async-done(((f32[4096,1024]{1,0:T(8,128)}), f32[32,1024]{1,0:T(8,128)}) %reduce-scatter.13.cloned.1.call-update) | async-done | bytes 131088 | tf_op jit(solution)/shard_map/reduce_scatter | solution.py:326
  (119 shorter events, 8.6 us)
Async XLA Ops:
  7.2 206.4 %all-gather.23.cloned.1.call-start = ((), (), s32[]{:S(2)}) async-start(), calls=%async_computation.8 | async-start | bytes 6340608 | tf_op jit(solution)/shard_map/all_gather | solution.py:281
  7.9 231.2 %all-gather.33.cloned.1.call-start = ((), (), s32[]{:S(2)}) async-start(), calls=%async_computation.13 | async-start | bytes 1556480 | tf_op jit(solution)/shard_map/all_gather | solution.py:67
  217.8 3.7 copy-start.27
  217.8 4.9 copy-start.28
  218.6 44.0 %all-gather.31.cloned.1.call-start = ((), (), s32[]{:S(2)}) async-start(), calls=%async_computation.12 | async-start | bytes 1556480 | tf_op jit(solution)/shard_map/all_gather | solution.py:68
  219.6 238.5 %all-gather.25.cloned.1.call-start = ((), (), s32[]{:S(2)}) async-start(), calls=%async_computation.9 | async-start | bytes 2113536 | tf_op jit(solution)/shard_map/all_gather | solution.py:283
  220.2 441.1 %all-gather.27.cloned.1.call-start = ((), (), s32[]{:S(2)}) async-start(), calls=%async_computation.10 | async-start | bytes 8454144 | tf_op jit(solution)/shard_map/all_gather | solution.py:287
  220.7 643.7 %all-gather.29.cloned.1.call-start = ((), (), s32[]{:S(2)}) async-start(), calls=%async_computation.11 | async-start | bytes 8454144 | tf_op jit(solution)/shard_map/all_gather | solution.py:289
  221.3 742.1 %all-reduce.24.cloned.1.call-start = ((), (), s32[]{:S(2)}) async-start(), calls=%async_computation.14 | async-start | bytes 5242880
  231.5 38.6 %copy-start.16 = (bf16[145,1024]{0,1:T(8,128)(2,1)}, bf16[145,1024]{0,1:T(8,128)(2,1)S(1)}, u32[]{:S(2)}) copy-start(bf16[145,1024]{0,1:T(8,128)(2,1)S(1)} %copy.58) | copy-start | bytes 890884
  246.6 24.8 copy-start.6
  270.1 3.2 copy-start.12
  271.5 2.7 copy-start
  274.2 183.9 %copy-start.5 = (bf16[1,145,1024]{2,1,0:T(8,128)(2,1)S(1)}, bf16[1,145,1024]{2,1,0:T(8,128)(2,1)}, u32[]{:S(2)}) copy-start(bf16[1,145,1024]{2,1,0:T(8,128)(2,1)} %param.15) | copy-start | bytes 890884
  276.1 395.7 %copy-start.20 = (bf16[16,64,145]{2,1,0:T(8,128)(2,1)}, bf16[16,64,145]{2,1,0:T(8,128)(2,1)S(1)}, u32[]{:S(2)}) copy-start(bf16[16,64,145]{2,1,0:T(8,128)(2,1)S(1)} %convolution_convert_fusion.1) | copy-start | bytes 890884
  460.3 418.4 %copy-start.3 = (f32[145,1024]{1,0:T(8,128)}, f32[145,1024]{1,0:T(8,128)S(1)}, u32[]{:S(2)}) copy-start(f32[145,1024]{1,0:T(8,128)S(1)} %get-tuple-element.98) | copy-start | bytes 1781764
  460.5 404.0 %copy-start.18 = (bf16[1,145,1024]{2,1,0:T(8,128)(2,1)S(1)}, bf16[1,145,1024]{2,1,0:T(8,128)(2,1)}, u32[]{:S(2)}) copy-start(bf16[1,145,1024]{2,1,0:T(8,128)(2,1)} %param.29) | copy-start | bytes 890884
  864.5 11.0 copy-start.8
  875.5 3.2 copy-start.14
  878.7 1.8 copy-start.9
  879.0 0.9 copy-start.10
  880.5 8.5 slice-start
  883.2 5.7 slice-start.1
  883.2 5.7 copy-start.13
  891.5 3.8 copy-start.17
  893.7 1.7 copy-start.1
  897.3 1.0 copy-start.21
  897.3 713.3 %reduce-scatter.9.cloned.1.call-start = ((), (), s32[]{:S(2)}) async-start(), calls=%async_computation.5 | async-start | bytes 4227072 | tf_op jit(solution)/shard_map/reduce_scatter | solution.py:320
  901.1 1.9 copy-start.2
  901.1 1366.0 %reduce-scatter.7.cloned.1.call-start = ((), (), s32[]{:S(2)}) async-start(), calls=%async_computation.4 | async-start | bytes 12681216 | tf_op jit(solution)/shard_map/reduce_scatter | solution.py:318
  965.0 1.6 copy-start.23
  966.6 0.8 copy-start.25
  975.0 1.1 copy-start.4
  975.0 1.5 copy-start.15
  975.0 1957.8 %reduce-scatter.11.cloned.1.call-start = ((), (), s32[]{:S(2)}) async-start(), calls=%async_computation.6 | async-start | bytes 16908288 | tf_op jit(solution)/shard_map/reduce_scatter | solution.py:324
  984.7 1.3 copy-start.7
  984.7 1.3 copy-start.19
  984.8 2613.7 %reduce-scatter.13.cloned.1.call-start = ((), (), s32[]{:S(2)}) async-start(), calls=%async_computation.7 | async-start | bytes 16908288 | tf_op jit(solution)/shard_map/reduce_scatter | solution.py:326
  994.3 5.7 copy-start.22
  994.3 5.7 copy-start.24
  994.3 5.7 copy-start.26
  1000.1 5.7 copy-start.11
Sparse Core Ops, SparseCore 0:
  9.7 203.8 all-gather.22
  218.7 20.3 all-gather.32
  241.3 21.2 all-gather.30
  264.2 193.8 all-gather.24
  459.6 201.6 all-gather.26
  662.9 201.5 all-gather.28
  897.4 65.9 all-reduce.23
  966.4 644.1 reduce-scatter.8
  1613.7 653.4 reduce-scatter.6
  2270.0 662.7 reduce-scatter.10
  2935.8 662.6 reduce-scatter.12
where the time goes:
time: 3610 us
  waiting for transfers between devices  3310 us (92%)
  blocking collectives  144 us (4%)
  matrix products  87.2 us (2%)
  local copies, waits for them, and re-layouts  39.9 us (1%)
    reduce_scatter x1, waiting for transfers between devices, body(): lax.psum_scatter(grad_reduce, ('dp', 'seq'), scatter_dimension=0, tiled=T...  666 us
    reduce_scatter x1, waiting for transfers between devices, body(): lax.psum_scatter(grad_expand, ('dp', 'seq'), scatter_dimension=0, tiled=T...  666 us
    reduce_scatter x1, waiting for transfers between devices, body(): lax.psum_scatter(grad_inward, ('dp', 'seq'), scatter_dimension=0, tiled=T...  657 us
    reduce_scatter x1, waiting for transfers between devices, body(): lax.psum_scatter(grad_outward, ('dp', 'seq'), scatter_dimension=0, tiled=...  533 us
    all_gather x1, waiting for transfers between devices, body(): lax.all_gather(up_weight[layer_index], ('dp', 'seq'), axis=0, tiled=True)  201 us
    all_gather x1, waiting for transfers between devices, body(): lax.all_gather(down_weight[layer_index], ('dp', 'seq'), axis=0, tiled=True)  193 us
    all_gather x1, waiting for transfers between devices, body(): lax.all_gather(output_weight[layer_index], ('dp', 'seq'), axis=0, tiled=T...  182 us
    unnamed x3, blocking collectives  144 us
  transfers between devices with their start and end apart: 11, of which 11 were waited for; matrix products, arithmetic and copies ran while one was open for 3% of the time, Pallas kernels for 0%

commit v1 on v0

v1 whole, which is shorter than its diff:
```python
import jax
import jax.numpy as jnp
from jax import lax
from jax.sharding import Mesh, PartitionSpec as P

HEADS = 16
HEAD_DIM = 64
TOK = 145
PAD = 160
LOCAL_HEADS = 4
GROUP = 4
WIDTH = 1024
BF = jnp.bfloat16
F32 = jnp.float32
DP = ("ylo", "z", "x")
SEQ = ("yhi", "core")
ALL = DP + SEQ
SWAP = [(0, 1), (1, 0)]


def over_y(v):
    return lax.ppermute(v, "yhi", SWAP)


def over_core(v):
    return lax.ppermute(v, "core", SWAP)


RELATIVE = (0, 2, 1, 3)


def gather_tokens(v):
    pair = jnp.stack([v, over_y(v)])
    return jnp.concatenate([pair, over_core(pair)])


def gather_heads(o):
    got = over_y(o)
    pair = jnp.stack([o, got[jnp.array([1, 0, 3, 2])]])
    other = over_core(pair)
    return jnp.concatenate([pair, other[:, jnp.array([2, 3, 0, 1])]])


def scatter_core(part):
    got = over_core(part[2:].astype(BF))
    return part[:2] + got.astype(F32)


def scatter_tokens(part):
    two = scatter_core(part)
    return two[0] + over_y(two[1].astype(BF)).astype(F32)


def rel_to_abs(v, seq_index):
    place = jnp.array([0, 2, 1, 3])
    return v[place[jnp.bitwise_xor(seq_index, jnp.arange(4))]]


def norm_stats(v):
    average = jnp.mean(v, axis=-1, keepdims=True)
    centred = v - average
    variance = jnp.mean(centred * centred, axis=-1, keepdims=True)
    scale = lax.rsqrt(variance + 1e-06)
    return centred * scale, scale


def norm_back(grad, gain, normed, scale):
    e = grad * gain
    return scale * (
        e
        - jnp.mean(e, axis=-1, keepdims=True)
        - normed * jnp.mean(e * normed, axis=-1, keepdims=True)
    )


def dot(a, b):
    return jnp.dot(a, b, preferred_element_type=F32)


def dot_t(a, b):
    return lax.dot_general(a, b, (((1,), (1,)), ((), ())), preferred_element_type=F32)


def t_dot(a, b):
    return lax.dot_general(a, b, (((0,), (0,)), ((), ())), preferred_element_type=F32)


def split_heads(v):
    return v.reshape(v.shape[0], LOCAL_HEADS, HEAD_DIM)


def body(
    inputs,
    token_mask,
    first_gain,
    first_shift,
    qkv_weight,
    qv_bias,
    out_weight,
    out_bias,
    second_gain,
    second_shift,
    up_weight,
    up_bias,
    down_weight,
    down_bias,
    cotangent,
):
    seq = lax.axis_index("yhi") * 2 + lax.axis_index("core")
    rows = GROUP * PAD

    down_pair = jnp.stack([down_weight[0], lax.ppermute(down_weight[0], "ylo", SWAP)])
    ylo = lax.axis_index("ylo")
    down_pair = jnp.where(ylo == 0, down_pair, down_pair[::-1])
    down_w = lax.all_gather(down_pair, ("z", "x"), axis=0, tiled=False).reshape(1024, WIDTH)

    mask_row = jnp.pad(token_mask.astype(BF), ((0, 0), (0, WIDTH - TOK)))
    x_block = jnp.concatenate(
        [inputs[0], mask_row, jnp.zeros((PAD - TOK - 1, WIDTH), BF)], axis=0
    )
    g_block = jnp.pad(cotangent[0], ((0, PAD - TOK), (0, 0)))
    both = gather_tokens(jnp.stack([x_block, g_block]))
    x_low, dm = both[:, 0].reshape(rows, WIDTH), both[:, 1].reshape(rows, WIDTH)
    keep = both[:, 0, TOK, :PAD].reshape(rows)

    qkv_cols = qkv_weight[0].reshape(8, 3, GROUP, 256).transpose(2, 0, 1, 3).reshape(GROUP, 8, 768)
    up_cols = (
        up_weight[0]
        .reshape(8, 2, 4, 4, GROUP, 32)
        .transpose(4, 0, 2, 3, 1, 5)
        .reshape(GROUP, 8, 1024)
    )
    out_cols = out_weight[0].reshape(8, GROUP, 256).transpose(1, 0, 2)
    extra = jnp.concatenate(
        [
            first_gain.reshape(8, 1),
            first_shift.reshape(8, 1),
            qv_bias.reshape(8, 2),
            out_bias.reshape(8, 1),
            second_gain.reshape(8, 1),
            second_shift.reshape(8, 1),
            up_bias.reshape(8, 4),
            down_bias.reshape(8, 1),
        ],
        axis=1,
    )
    extra = jnp.broadcast_to(jnp.pad(extra, ((0, 0), (0, 116)))[None], (GROUP, 8, 128))
    piece = jnp.concatenate([qkv_cols, up_cols, out_cols, extra], axis=2)
    send = jnp.broadcast_to(piece[None], (32, GROUP, 8, 2176)).reshape(1024, 2176)
    got = lax.all_to_all(send, ALL, 0, 0, tiled=True)
    qkv_w = got[:, :768]
    up_w = got[:, 768:1792]
    out_mine = got[:, 1792:2048]
    vectors = got[:, 2048:2060].astype(F32)
    gain_1, shift_1 = vectors[:, 0], vectors[:, 1]
    q_bias = lax.dynamic_slice(vectors[:, 2:4].reshape(2048), (seq * 256,), (256,))
    v_bias = lax.dynamic_slice(vectors[:, 2:4].reshape(2048), (1024 + seq * 256,), (256,))
    b_out, gain_2, shift_2 = vectors[:, 4], vectors[:, 5], vectors[:, 6]
    b_up = vectors[:, 7:11].reshape(2, 4, 4, GROUP, 32)
    b_up = lax.dynamic_index_in_dim(b_up, seq, 3, keepdims=False).transpose(1, 2, 0, 3).reshape(1024)
    b_down = vectors[:, 11]

    out_w = rel_to_abs(gather_tokens(out_mine), seq)
    out_w = out_w.reshape(GROUP, GROUP, 256, 256)[:, jnp.bitwise_xor(seq, jnp.array(RELATIVE))]
    out_w = out_w.transpose(1, 2, 0, 3).reshape(WIDTH, WIDTH)

    x = x_low.astype(F32)
    normed_1, scale_1 = norm_stats(x)
    n1 = (normed_1 * gain_1 + shift_1).astype(BF)
    proj = dot(n1, qkv_w)
    q = split_heads((proj[:, :256] + q_bias).astype(BF))
    k = split_heads(proj[:, 256:512].astype(BF))
    v = split_heads((proj[:, 512:] + v_bias).astype(BF))
    scores = jnp.einsum("qhd,khd->hqk", q, k, preferred_element_type=F32) * HEAD_DIM ** (-0.5)
    scores = jnp.where(keep[None, None, :] > 0, scores, -1e30)
    peak = jnp.max(scores, axis=-1, keepdims=True)
    lse = peak + jnp.log(jnp.sum(jnp.exp(scores - peak), axis=-1, keepdims=True))
    probs = jnp.exp(scores - lse)
    probs_low = probs.astype(BF)
    o = jnp.einsum("hqk,khd->qhd", probs_low, v, preferred_element_type=F32)
    o = o.astype(BF).reshape(GROUP, PAD, 256)
    o_all = gather_heads(o).transpose(1, 2, 0, 3).reshape(rows, WIDTH)
    r = x + dot(o_all, out_w) + b_out
    normed_2, scale_2 = norm_stats(r)
    n2 = (normed_2 * gain_2 + shift_2).astype(BF)
    u = dot(n2, up_w) + b_up
    cdf = 0.5 * (1.0 + lax.erf(u * (0.5**0.5)))
    z = (u * cdf).astype(BF)
    slope = cdf + u * jnp.exp(-0.5 * u * u) * 0.3989422804014327
    y_part = dot(z, down_w).reshape(GROUP, PAD, WIDTH)
    y = scatter_tokens(y_part) + r[:PAD] + b_down
    block_output = y[:TOK].astype(BF)[None]

    d_down_w = t_dot(z, dm)
    d_down_w = lax.psum_scatter(
        d_down_w.astype(BF).reshape(16, 64, WIDTH), ("z", "x"), scatter_dimension=0, tiled=True
    )[0].reshape(2, 32, WIDTH)
    mine = jnp.where(ylo == 0, d_down_w[0], d_down_w[1])
    theirs = jnp.where(ylo == 0, d_down_w[1], d_down_w[0])
    d_down_w = mine.astype(F32) + lax.ppermute(theirs, "ylo", SWAP).astype(F32)
    du = (slope * dot_t(dm, down_w)).astype(BF)
    d_up_w = t_dot(n2, du)
    d_up_b = jnp.sum(du, axis=0, dtype=F32)
    dn2 = dot_t(du, up_w).reshape(GROUP, PAD, WIDTH)
    two = scatter_core(dn2).astype(BF)
    dn2 = (two.astype(F32) + over_y(two).astype(F32)[::-1]).reshape(2 * PAD, WIDTH)
    half = 2 * PAD
    dr = dm[:half].astype(F32) + norm_back(dn2, gain_2, normed_2[:half], scale_2[:half])
    da = dr.astype(BF)
    da = jnp.concatenate([da, over_core(da)])
    d_gain_2 = jnp.sum(dn2[:PAD] * normed_2[:PAD], axis=0)
    d_shift_2 = jnp.sum(dn2[:PAD], axis=0)
    d_out_b = jnp.sum(da[:PAD], axis=0, dtype=F32)
    d_down_b = jnp.sum(dm[:PAD], axis=0, dtype=F32)
    d_out_w = t_dot(o_all, lax.dynamic_slice(da, (0, seq * 256), (rows, 256))).astype(BF)
    d_out_w = rel_to_abs(d_out_w.reshape(GROUP, 256, 256), seq).reshape(WIDTH, 256)
    do = split_heads(dot_t(da, out_w[:256]).astype(BF))
    d_probs = jnp.einsum("qhd,khd->hqk", do, v, preferred_element_type=F32)
    inner = jnp.sum(probs * d_probs, axis=-1, keepdims=True)
    ds = (probs * (d_probs - inner)).astype(BF)
    dq = jnp.einsum("hqk,khd->qhd", ds, k, preferred_element_type=F32) * HEAD_DIM ** (-0.5)
    dk = jnp.einsum("hqk,qhd->khd", ds, q, preferred_element_type=F32) * HEAD_DIM ** (-0.5)
    dv = jnp.einsum("hqk,qhd->khd", probs_low, do, preferred_element_type=F32)
    d_proj = jnp.concatenate([t.astype(BF).reshape(rows, 256) for t in (dq, dk, dv)], axis=1)
    d_bias = jnp.sum(d_proj, axis=0, dtype=F32)
    d_qkv_w = t_dot(n1, d_proj)
    dn1 = dot_t(d_proj, qkv_w)
    d_gain_1 = jnp.sum(dn1 * normed_1, axis=0)
    d_shift_1 = jnp.sum(dn1, axis=0)

    own = (jnp.arange(GROUP) == seq).astype(F32)
    d_qv_b = jnp.concatenate(
        [(own[:, None] * d_bias[None, :256]).reshape(-1), (own[:, None] * d_bias[None, 512:]).reshape(-1)]
    )
    d_up_b = d_up_b.reshape(4, 4, 2, 32).transpose(2, 0, 1, 3).reshape(32, 1, 32)
    d_up_b = (d_up_b * own[None, :, None]).reshape(1024, 4)
    extra = jnp.concatenate(
        [
            jnp.stack([d_gain_1, d_shift_1], axis=1),
            d_qv_b.reshape(1024, 2),
            jnp.stack([d_out_b, d_gain_2, d_shift_2], axis=1),
            d_up_b,
            d_down_b.reshape(1024, 1),
            jnp.zeros((1024, 116), F32),
        ],
        axis=1,
    )
    send = jnp.concatenate(
        [d_qkv_w.astype(BF), d_up_w.astype(BF), d_out_w, extra.astype(BF)], axis=1
    )
    got = lax.all_to_all(send, ALL, 0, 0, tiled=True)
    total = jnp.sum(got.reshape(32, GROUP, 8, 2176).astype(F32), axis=0)
    d_qkv_w = total[:, :, :768].reshape(GROUP, 8, 3, 256).transpose(1, 2, 0, 3).reshape(1, 8, 3072)
    d_up_w = (
        total[:, :, 768:1792]
        .reshape(GROUP, 8, 4, 4, 2, 32)
        .transpose(1, 4, 2, 3, 0, 5)
        .reshape(1, 8, 4096)
    )
    d_out_w = total[:, :, 1792:2048].transpose(1, 0, 2).reshape(1, 8, WIDTH)
    small = jnp.sum(total[:, :, 2048:2060], axis=0)

    def column(i):
        return small[:, i].reshape(1, 8)

    dn1_own = scatter_tokens(dn1.reshape(GROUP, PAD, WIDTH))
    g0 = dr[:PAD] + norm_back(dn1_own, gain_1, normed_1[:PAD], scale_1[:PAD])
    return (
        block_output,
        g0[:TOK][None],
        column(0),
        column(1),
        d_qkv_w,
        small[:, 2:4].reshape(1, 16),
        d_out_w,
        column(4),
        column(5),
        column(6),
        d_up_w,
        small[:, 7:11].reshape(1, 32),
        d_down_w[None],
        column(11),
    )


def solution(mesh):
    fine = Mesh(mesh.devices.reshape(2, 4, 4, 2, 2), ALL)
    tokens = P(DP, SEQ, None)
    vector = P(None, ALL)
    matrix = P(None, ALL, None)
    return jax.shard_map(
        body,
        mesh=fine,
        in_specs=(
            tokens,
            P(DP, SEQ),
            vector,
            vector,
            matrix,
            vector,
            matrix,
            vector,
            vector,
            vector,
            matrix,
            vector,
            matrix,
            vector,
            tokens,
        ),
        out_specs=(
            tokens,
            tokens,
            vector,
            vector,
            matrix,
            vector,
            matrix,
            vector,
            vector,
            vector,
            matrix,
            vector,
            matrix,
            vector,
        ),
        check_vma=False,
    )
```

time: 3610 us -> 473 us (0.13)
  waiting for transfers between devices: 3310 us -> 193 us
  blocking collectives: 144 us -> 0 us
  local copies, waits for them, and re-layouts: 39.9 us -> 103 us
  other arithmetic: 10.3 us -> 55.7 us
  starting transfers between devices: 0.61 us -> 41 us
    reduce_scatter x4 -> x0, waiting for transfers between devices: 2520 us -> none  [the longest x1 666 us: body(): lax.psum_scatter(grad_reduce, ('dp', 'seq'), scatter_dimension=0, tiled=T...]
    all_gather x6 -> x1, waiting for transfers between devices: 727 us -> 0.01 us  [body(): lax.all_gather(down_pair, ('z', 'x'), axis=0, tiled=False)]
    unnamed x3 -> x0, blocking collectives: 144 us -> none
    ppermute x0 -> x15, waiting for transfers between devices: none -> 78.8 us  [the longest x6 74.5 us: over_y(): return lax.ppermute(v, 'yhi', SWAP)]
    unnamed x12 -> x3, waiting for transfers between devices: 59.4 us -> 114 us
  transfers between devices with their start and end apart: 11 -> 19, of which waited for: 11 -> 7; matrix products, arithmetic and copies ran while one was open for 3% -> 27% of each run, Pallas kernels for 0% -> 0%
where the time goes in v1:
time: 473 us; the launch traced here: 465 us
  waiting for transfers between devices  193 us (41%)
  local copies, waits for them, and re-layouts  103 us (22%)
  matrix products  56.4 us (12%)
  other arithmetic  55.7 us (12%)
  starting transfers between devices  41 us (9%)
  between operations  15.3 us (3%)
    unnamed x3, waiting for transfers between devices  114 us
    ppermute x6, waiting for transfers between devices, over_y(): return lax.ppermute(v, 'yhi', SWAP)  74.5 us
    all_to_all x2, starting transfers between devices, body(): got = lax.all_to_all(send, ALL, 0, 0, tiled=True)  23.3 us
    dot_general x4, matrix products, dot_t(): lax.dot_general(a, b, (((1,), (1,)), ((), ())), preferred_element_type=F32)  16.6 us
    unnamed x125, local copies, waits for them, and re-layouts  14.8 us
    ppermute x6, starting transfers between devices, over_y(): return lax.ppermute(v, 'yhi', SWAP)  13.9 us
    dot_general x4, matrix products, t_dot(): lax.dot_general(a, b, (((0,), (0,)), ((), ())), preferred_element_type=F32)  13 us
    dot_general x4, matrix products, dot(): return jnp.dot(a, b, preferred_element_type=F32)  12.7 us
  transfers between devices with their start and end apart: 19, of which 7 were waited for; matrix products, arithmetic and copies ran while one was open for 27% of the time, Pallas kernels for 0%

profile of v1, /device:TPU:0, one launch (start us, length us, event | category | flops | bytes accessed | tf_op | source)
XLA Modules:
  0.0 464.7 jit_solution(17243707541315224797)
XLA Ops:
  18.4 2.4 broadcast_in_dim.34
  20.7 11.6 %all-to-all-start = ((bf16[128,8,2176]{2,1,0:T(8,128)(2,1)}), bf16[128,8,2176]{2,1,0:T(8,128)(2,1)}, u32[]{:S(2)}, u32[]{:S(2)}) async-start(bf16[128,8,2176]{2,1,0:T(8,128)(2,1)} %bitcast.203), calls=%async_computation | async-start | bytes 8912896 | tf_op jit(solution)/shard_map/all_to_all | solution.py:150
  32.8 2.5 collective-permute-start
  35.2 62.5 %collective-permute-done = bf16[2,160,1024]{2,1,0:T(8,128)(2,1)S(1)} collective-permute-done((bf16[2,160,1024]{2,1,0:T(8,128)(2,1)S(1)}, bf16[2,160,1024]{2,1,0:T(8,128)(2,1)S(1)}, u32[]{:S(2)}, u32[]{:S(2)}) %collective-permute-start) | collective-permute-done | bytes 655392 | tf_op jit(solution)/shard_map/ppermute | solution.py:22
  100.2 3.4 collective-permute-done.6
  105.5 1.7 pad_maximum_fusion
  108.2 1.8 fusion.10
  111.0 1.9 slice_reduce_fusion.1
  113.9 2.1 slice_bitcast_fusion.2
  117.3 2.2 collective-permute-start.4
  119.5 3.4 fusion.19
  125.9 2.0 copy.174
  127.9 2.5 fusion
  133.1 3.3 fusion.1
  137.6 3.4 fusion.25
  141.0 2.2 reshape.454
  143.2 2.0 copy.176
  145.2 2.1 collective-permute-start.2
  147.4 2.3 pad_maximum_fusion.7
  150.3 2.1 stack_reshape.3
  152.4 2.0 copy.177
  154.5 1.9 collective-permute-done.2
  156.3 1.5 gather_fusion
  157.9 1.9 pad_maximum_fusion.10
  161.1 1.9 fusion.60
  166.7 2.6 gather_fusion.1
  173.0 2.9 pad_maximum_fusion.1
  175.9 3.7 gather_fusion.3
  179.6 3.7 gather_fusion.4
  183.3 3.2 copy.181
  188.2 1.7 fusion.63
  191.4 1.5 copy-done.7
  192.9 4.8 %multiply_convert_fusion.1 = (bf16[640,1024]{1,0:T(8,128)(2,1)}, f32[640,1024]{1,0:T(8,128)}) fusion(f32[1024]{0:T(1024)S(1)} %add.237, bf16[1024,2176]{1,0:T(8,128)(2,1)} %bitcast.19, f32[640,1024]{1,0:T(8,128)S(1)} %subtract_multiply_fusion, f32[1024]{0:T(1024)S(1)} %copy-done.46, f32[1024]{0:T(1024)S(1)} %get-tuple-element.90), kind=kOutput, calls=%fused_computation.32 | convolution fusion | flops 1348075520 | bytes 8663040 | tf_op jit(solution)/shard_map/dot_general | solution.py:77
  197.7 5.7 %convert_reduce_fusion.2 = (f32[1024]{0:T(1024)}, bf16[640,1024]{1,0:T(8,128)(2,1)S(1)}) fusion(bf16[640,1024]{1,0:T(8,128)(2,1)} %bitcast.229, bf16[1024,1024]{1,0:T(8,128)(2,1)} %bitcast.278, f32[640,1024]{1,0:T(8,128)} %get-tuple-element.127, f32[1024]{0:T(1024)S(1)} %add.237), kind=kOutput, calls=%fused_computation.30 | convolution fusion | flops 1350695936 | bytes 7348224 | tf_op jit(solution)/shard_map/dot_general | solution.py:81
  203.4 3.7 fusion.12
  212.6 2.2 add_convert_fusion.2
  214.8 1.9 collective-permute-start.10
  219.8 1.9 fusion.26
  226.7 6.6 %collective-permute-done.10 = bf16[2,160,1024]{2,1,0:T(8,128)(2,1)} collective-permute-done((bf16[2,160,1024]{2,1,0:T(8,128)(2,1)}, bf16[2,160,1024]{2,1,0:T(8,128)(2,1)}, u32[]{:S(2)}, u32[]{:S(2)}) %collective-permute-start.10) | collective-permute-done | bytes 655392 | tf_op jit(solution)/shard_map/ppermute | solution.py:22
  234.5 2.3 multiply_reduce_fusion.4
  237.5 1.6 bitcast_multiply_fusion
  240.2 1.5 fusion.59
  241.7 3.2 convert_bitcast_fusion
  249.9 2.0 fusion.24
  253.4 5.3 %multiply_reduce_fusion = (f32[4,640]{1,0:T(4,128)S(1)}, f32[4,640,640]{1,2,0:T(8,128)S(1)}) fusion(f32[4,640,640]{1,2,0:T(8,128)} %copy-done.1, f32[4,640]{1,0:T(4,128)S(1)} %log_add_fusion, pred[640]{0:T(1024)(128)(4,1)S(1)} %copy-done.32, bf16[640,4,64]{0,2,1:T(8,128)(2,1)S(1)} %bitcast.232, bf16[640,4,64]{0,2,1:T(8,128)(2,1)S(1)} %bitcast.221), kind=kOutput, calls=%fused_computation.8 | convolution fusion | flops 217904640 | bytes 13783680 | tf_op jit(solution)/shard_map/qhd,khd->hqk/dot_general | solution.py:218
  258.7 2.5 multiply_convert_fusion
  263.1 5.2 %fusion.56 = (bf16[1024]{0:T(1024)(128)(2,1)}, bf16[1024]{0:T(1024)(128)(2,1)S(1)}, f32[640,1024]{1,0:T(8,128)}) fusion(f32[640]{0:T(1024)S(1)} %copy-done.41, f32[640]{0:T(1024)S(1)} %copy-done.39, bf16[4,2,160,1024]{3,2,1,0:T(8,128)(2,1)S(1)} %pad_maximum_fusion, bf16[1024,2176]{1,0:T(8,128)(2,1)} %bitcast.19, bf16[640,256]{0,1:T(8,128)(2,1)S(1)} %bitcast.235, ...), kind=kOutput, calls=%fused_computation.182 | convolution fusion | flops 1013512192 | bytes 6497280 | tf_op jit(solution)/shard_map/dot_general | solution.py:81
  268.5 2.6 fusion.16
  271.2 2.5 convolution_convert_fusion.2
  273.7 1.7 gather_fusion.5
  279.2 8.0 %concatenate.80 = bf16[128,8,2176]{2,1,0:T(8,128)(2,1)} concatenate(bf16[128,8,768]{2,1,0:T(8,128)(2,1)} %fusion.16, bf16[128,8,1024]{2,1,0:T(8,128)(2,1)S(1)} %copy-done.21, bf16[128,8,256]{2,1,0:T(8,128)(2,1)S(1)} %bitcast.228, bf16[128,8,1]{2,1,0:T(8,128)(2,1)} %concatenate.81, bf16[128,8,1]{2,1,0:T(8,128)(2,1)S(1)} %concatenate.82, bf16[128,8,2]{2,1,0:T(8,128)(2,1)S(1)} %bitcast.244, ...), dimensions={2} | concatenate | bytes 8912896 | tf_op jit(solution)/shard_map/concatenate | solution.py:248
  287.2 11.7 %all-to-all-start.1 = ((bf16[128,8,2176]{2,1,0:T(8,128)(2,1)}), bf16[128,8,2176]{2,1,0:T(8,128)(2,1)}, u32[]{:S(2)}, u32[]{:S(2)}) async-start(bf16[128,8,2176]{2,1,0:T(8,128)(2,1)} %concatenate.80), calls=%async_computation.1 | async-start | bytes 8912896 | tf_op jit(solution)/shard_map/all_to_all | solution.py:251
  299.0 4.7 %convolution_convert_fusion = bf16[1024,1024]{1,0:T(8,128)(2,1)} fusion(bf16[640,1024]{1,0:T(8,128)(2,1)} %get-tuple-element.126, bf16[640,1024]{1,0:T(8,128)(2,1)S(1)} %bitcast.230), kind=kOutput, calls=%fused_computation.41 | convolution fusion | flops 1343225856 | bytes 4718592 | tf_op jit(solution)/shard_map/dot_general | solution.py:85
  303.7 2.8 fusion.64
  306.5 1.5 copy-done.23
  314.5 2.4 collective-permute-start.8
  317.1 114.4 %all-reduce.6.cloned.1.call-done = bf16[16,64,1024]{2,1,0:T(8,128)(2,1)} async-done(((bf16[16,64,1024]{2,1,0:T(8,128)(2,1)}), bf16[16,64,1024]{2,1,0:T(8,128)(2,1)}) %all-reduce.6.cloned.1.call-update) | async-done | bytes 2097168
  431.5 1.6 select_bitcast_fusion
  433.0 1.6 collective-permute-start.14
  436.0 2.8 collective-permute-start.13
  438.8 1.8 fusion.46
  440.7 2.2 fusion.47
  442.9 3.5 collective-permute-done.13
  449.4 3.0 convert_reduce_fusion
  (291 shorter events, 84.3 us)
Async XLA Ops:
  20.7 11.7 %copy-start.50 = (s32[1,145]{1,0:T(1,128)S(1)}, s32[1,145]{1,0:T(1,128)}, u32[]{:S(2)}) copy-start(s32[1,145]{1,0:T(1,128)} %param.21) | copy-start | bytes 1744
  20.7 11.8 %copy-start.28 = (bf16[1,145,1024]{2,1,0:T(8,128)(2,1)S(1)}, bf16[1,145,1024]{2,1,0:T(8,128)(2,1)}, u32[]{:S(2)}) copy-start(bf16[1,145,1024]{2,1,0:T(8,128)(2,1)} %param.20) | copy-start | bytes 890884
  20.7 11.8 %copy-start.29 = (bf16[1,145,1024]{2,1,0:T(8,128)(2,1)S(1)}, bf16[1,145,1024]{2,1,0:T(8,128)(2,1)}, u32[]{:S(2)}) copy-start(bf16[1,145,1024]{2,1,0:T(8,128)(2,1)} %param.34) | copy-start | bytes 890884
  20.7 89.3 %all-to-all-start = ((bf16[128,8,2176]{2,1,0:T(8,128)(2,1)}), bf16[128,8,2176]{2,1,0:T(8,128)(2,1)}, u32[]{:S(2)}, u32[]{:S(2)}) async-start(bf16[128,8,2176]{2,1,0:T(8,128)(2,1)} %bitcast.203), calls=%async_computation | async-start | bytes 8912896 | tf_op jit(solution)/shard_map/all_to_all | solution.py:150
  32.3 165.4 %all-gather.3.cloned.1.call-start = ((), (), s32[]{:S(2)}) async-start(), calls=%async_computation.2 | async-start | bytes 2228224 | tf_op jit(solution)/shard_map/all_gather | solution.py:115
  32.5 66.6 %copy-start.30 = (bf16[1,32,1024]{2,1,0:T(8,128)(2,1)S(1)}, bf16[1,32,1024]{2,1,0:T(8,128)(2,1)}, u32[]{:S(2)}) copy-start(bf16[1,32,1024]{2,1,0:T(8,128)(2,1)} %param.32) | copy-start | bytes 196612
  32.6 66.9 %copy-start = (s32[4]{0:T(128)S(1)}, s32[4]{0:T(128)}, u32[]{:S(2)}) copy-start(s32[4]{0:T(128)} %constant.74.clone) | copy-start | bytes 52
  32.7 72.8 %copy-start.4 = (bf16[1,2,160,1024]{3,2,1,0:T(8,128)(2,1)}, bf16[1,2,160,1024]{3,2,1,0:T(8,128)(2,1)S(1)}, u32[]{:S(2)}) copy-start(bf16[1,2,160,1024]{3,2,1,0:T(8,128)(2,1)S(1)} %get-tuple-element.112) | copy-start | bytes 1966084
  32.8 65.0 %collective-permute-start = (bf16[2,160,1024]{2,1,0:T(8,128)(2,1)S(1)}, bf16[2,160,1024]{2,1,0:T(8,128)(2,1)S(1)}, u32[]{:S(2)}, u32[]{:S(2)}) collective-permute-start(bf16[2,160,1024]{2,1,0:T(8,128)(2,1)S(1)} %get-tuple-element.113), channel_id=1, source_target_pairs={{0,2},{2,0},{1,3},{3,1},{4,6},{6,4},{5,7},{7,5},{8,10},{10,8},{9,1... | collective-permute-start | bytes 1966088 | tf_op jit(solution)/shard_map/ppermute | solution.py:22
  97.8 6.6 %copy-start.9 = (bf16[2,160,1024]{2,1,0:T(8,128)(2,1)}, bf16[2,160,1024]{2,1,0:T(8,128)(2,1)S(1)}, u32[]{:S(2)}) copy-start(bf16[2,160,1024]{2,1,0:T(8,128)(2,1)S(1)} %collective-permute-done) | copy-start | bytes 1966084
  99.1 5.2 %collective-permute-start.1 = (bf16[2,2,160,1024]{3,2,1,0:T(8,128)(2,1)}, bf16[2,2,160,1024]{3,2,1,0:T(8,128)(2,1)S(1)}, u32[]{:S(2)}, u32[]{:S(2)}) collective-permute-start(bf16[2,2,160,1024]{3,2,1,0:T(8,128)(2,1)} %pad_maximum_fusion.2), channel_id=1, source_target_pairs={{0,1},{1,0},{2,3},{3,2},{4,5},{5,4},{6,7},{7,6},{8,9},{9,8},{10,11... | collective-permute-start | bytes 3932168 | tf_op jit(solution)/shard_map/ppermute | solution.py:26
  99.1 4.5 collective-permute-start.6
  105.5 26.4 %copy-start.31 = (pred[640]{0:T(1024)(128)(4,1)}, pred[640]{0:T(1024)(128)(4,1)S(1)}, u32[]{:S(2)}) copy-start(pred[640]{0:T(1024)(128)(4,1)S(1)} %gt.16) | copy-start | bytes 1924
  107.6 2.4 copy-start.38
  108.1 1.9 copy-start.34
  108.2 1.8 copy-start.40
  112.9 10.0 %copy-start.35 = (f32[1024]{0:T(1024)}, f32[1024]{0:T(1024)S(1)}, u32[]{:S(2)}) copy-start(f32[1024]{0:T(1024)S(1)} %get-tuple-element.93) | copy-start | bytes 12292
  112.9 10.0 %copy-start.44 = (f32[1024]{0:T(1024)}, f32[1024]{0:T(1024)S(1)}, u32[]{:S(2)}) copy-start(f32[1024]{0:T(1024)S(1)} %get-tuple-element.92) | copy-start | bytes 12292
  117.3 30.0 %collective-permute-start.4 = (bf16[1024,256]{1,0:T(8,128)(2,1)}, bf16[1024,256]{1,0:T(8,128)(2,1)}, u32[]{:S(2)}, u32[]{:S(2)}) collective-permute-start(bf16[1024,256]{1,0:T(8,128)(2,1)} %get-tuple-element.106), channel_id=1, source_target_pairs={{0,2},{2,0},{1,3},{3,1},{4,6},{6,4},{5,7},{7,5},{8,10},{10,8},{9,1... | collective-permute-start | bytes 1572872 | tf_op jit(solution)/shard_map/ppermute | solution.py:22
  125.9 4.5 copy-start.14
  130.4 2.7 copy-start.1
  137.6 7.6 %copy-start.17 = (bf16[640,256]{0,1:T(8,128)(2,1)}, bf16[640,256]{0,1:T(8,128)(2,1)S(1)}, u32[]{:S(2)}) copy-start(bf16[640,256]{0,1:T(8,128)(2,1)S(1)} %copy.172) | copy-start | bytes 983044
  141.0 9.2 %copy-start.52 = (s32[4]{0:T(128)S(1)}, s32[4]{0:T(128)}, u32[]{:S(2)}) copy-start(s32[4]{0:T(128)} %constant.108) | copy-start | bytes 52
  145.2 11.1 %collective-permute-start.2 = (bf16[4,160,256]{2,1,0:T(8,128)(2,1)}, bf16[4,160,256]{2,1,0:T(8,128)(2,1)}, u32[]{:S(2)}, u32[]{:S(2)}) collective-permute-start(bf16[4,160,256]{2,1,0:T(8,128)(2,1)} %copy.176), channel_id=1, source_target_pairs={{0,2},{2,0},{1,3},{3,1},{4,6},{6,4},{5,7},{7,5},{8,10},{10,8},{9,1... | collective-permute-start | bytes 983048 | tf_op jit(solution)/shard_map/ppermute | solution.py:22
  147.4 13.2 %copy-start.51 = (s32[4]{0:T(128)S(1)}, s32[4]{0:T(128)}, u32[]{:S(2)}) copy-start(s32[4]{0:T(128)} %constant.109) | copy-start | bytes 52
  149.7 23.3 %collective-permute-start.5 = (bf16[2,1024,256]{2,1,0:T(8,128)(2,1)}, bf16[2,1024,256]{2,1,0:T(8,128)(2,1)}, u32[]{:S(2)}, u32[]{:S(2)}) collective-permute-start(bf16[2,1024,256]{2,1,0:T(8,128)(2,1)} %pad_maximum_fusion.7), channel_id=1, source_target_pairs={{0,1},{1,0},{2,3},{3,2},{4,5},{5,4},{6,7},{7,6},{8,9},{9,8},{10,11... | collective-permute-start | bytes 3145736 | tf_op jit(solution)/shard_map/ppermute | solution.py:26
  159.8 7.0 %collective-permute-start.3 = (bf16[2,4,160,256]{3,2,1,0:T(8,128)(2,1)}, bf16[2,4,160,256]{3,2,1,0:T(8,128)(2,1)}, u32[]{:S(2)}, u32[]{:S(2)}) collective-permute-start(bf16[2,4,160,256]{3,2,1,0:T(8,128)(2,1)} %pad_maximum_fusion.10), channel_id=1, source_target_pairs={{0,1},{1,0},{2,3},{3,2},{4,5},{5,4},{6,7},{7,6},{8,9},{9,8},{10,11... | collective-permute-start | bytes 1966088 | tf_op jit(solution)/shard_map/ppermute | solution.py:26
  170.6 2.4 copy-start.12
  186.5 1.7 copy-start.26
  190.3 2.6 copy-start.46
  203.4 3.7 copy-start.55
  209.5 2.7 collective-permute-start.9
  211.3 5.4 %copy-start.5 = (bf16[1,2,160,1024]{3,2,1,0:T(8,128)(2,1)S(1)}, bf16[1,2,160,1024]{3,2,1,0:T(8,128)(2,1)}, u32[]{:S(2)}) copy-start(bf16[1,2,160,1024]{3,2,1,0:T(8,128)(2,1)} %copy-done.4) | copy-start | bytes 1966084
  214.8 18.5 %collective-permute-start.10 = (bf16[2,160,1024]{2,1,0:T(8,128)(2,1)}, bf16[2,160,1024]{2,1,0:T(8,128)(2,1)}, u32[]{:S(2)}, u32[]{:S(2)}) collective-permute-start(bf16[2,160,1024]{2,1,0:T(8,128)(2,1)} %add_convert_fusion.2), channel_id=1, source_target_pairs={{0,2},{2,0},{1,3},{3,1},{4,6},{6,4},{5,7},{7,5},{8,10},{10,8},{9,1... | collective-permute-start | bytes 1966088 | tf_op jit(solution)/shard_map/ppermute | solution.py:22
  237.5 2.1 copy-start.8
  237.5 2.5 copy-start.3
  237.5 2.7 copy-start.20
  237.5 2.7 slice-start.3
  237.5 2.7 copy-start.42
  241.7 8.2 %collective-permute-start.11 = (bf16[320,1024]{1,0:T(8,128)(2,1)S(1)}, bf16[320,1024]{1,0:T(8,128)(2,1)}, u32[]{:S(2)}, u32[]{:S(2)}) collective-permute-start(bf16[320,1024]{1,0:T(8,128)(2,1)S(1)} %get-tuple-element.101), channel_id=1, source_target_pairs={{0,1},{1,0},{2,3},{3,2},{4,5},{5,4},{6,7},{7,6},{8,9},{9,8},{10,11... | collective-permute-start | bytes 1966088 | tf_op jit(solution)/shard_map/ppermute | solution.py:26
  249.9 2.3 copy-start.2
  252.2 6.5 %slice-start = ((s8[6553600]{0:T(1024)(128)(4,1)}), s8[4194304]{0:T(1024)(128)(4,1)S(1)}, s32[]{:S(2)}) async-start(s8[6553600]{0:T(1024)(128)(4,1)} %bitcast.201), calls=%async_computation.4 | async-start | bytes 8388608
  253.4 5.3 %slice-start.1 = ((s8[6553600]{0:T(1024)(128)(4,1)}), s8[2359296]{0:T(1024)(128)(4,1)S(1)}, s32[]{:S(2)}) async-start(s8[6553600]{0:T(1024)(128)(4,1)} %bitcast.201), calls=%async_computation.5 | async-start | bytes 4718592
  258.7 2.6 copy-start.15
  263.1 5.4 %copy-start.13 = (f32[640,1024]{1,0:T(8,128)S(1)}, f32[640,1024]{1,0:T(8,128)}, u32[]{:S(2)}) copy-start(f32[640,1024]{1,0:T(8,128)} %fusion.10) | copy-start | bytes 7864324
  263.1 5.4 %copy-start.36 = (f32[1024]{0:T(1024)S(1)}, f32[1024]{0:T(1024)}, u32[]{:S(2)}) copy-start(f32[1024]{0:T(1024)} %copy-done.35) | copy-start | bytes 12292
  263.1 5.4 %copy-start.45 = (f32[1024]{0:T(1024)S(1)}, f32[1024]{0:T(1024)}, u32[]{:S(2)}) copy-start(f32[1024]{0:T(1024)} %copy-done.44) | copy-start | bytes 12292
  268.5 2.6 copy-start.27
  271.2 4.7 %copy-start.43 = (f32[512]{0:T(512)S(1)}, f32[512]{0:T(512)}, u32[]{:S(2)}) copy-start(f32[512]{0:T(512)} %broadcast_bitcast_fusion.2) | copy-start | bytes 6148
  271.2 8.0 %copy-start.21 = (bf16[128,8,1024]{2,1,0:T(8,128)(2,1)S(1)}, bf16[128,8,1024]{2,1,0:T(8,128)(2,1)}, u32[]{:S(2)}) copy-start(bf16[128,8,1024]{2,1,0:T(8,128)(2,1)} %convert_bitcast_fusion) | copy-start | bytes 6291460
  287.2 11.8 %copy-start.24 = (bf16[4,1,160,1024]{3,2,1,0:T(8,128)(2,1)S(1)}, bf16[4,1,160,1024]{3,2,1,0:T(8,128)(2,1)}, u32[]{:S(2)}) copy-start(bf16[4,1,160,1024]{3,2,1,0:T(8,128)(2,1)} %get-tuple-element.108) | copy-start | bytes 3932164
  287.2 162.3 %all-to-all-start.1 = ((bf16[128,8,2176]{2,1,0:T(8,128)(2,1)}), bf16[128,8,2176]{2,1,0:T(8,128)(2,1)}, u32[]{:S(2)}, u32[]{:S(2)}) async-start(bf16[128,8,2176]{2,1,0:T(8,128)(2,1)} %concatenate.80), calls=%async_computation.1 | async-start | bytes 8912896 | tf_op jit(solution)/shard_map/all_to_all | solution.py:251
  298.9 132.6 %all-reduce.6.cloned.1.call-start = ((), (), s32[]{:S(2)}) async-start(), calls=%async_computation.3 | async-start | bytes 4194304
  299.0 4.7 %copy-start.53 = (bf16[32,32,1024]{2,1,0:T(8,128)(2,1)S(1)}, bf16[32,32,1024]{2,1,0:T(8,128)(2,1)}, u32[]{:S(2)}) copy-start(bf16[32,32,1024]{2,1,0:T(8,128)(2,1)} %all-gather.3.cloned.1.call-done) | copy-start | bytes 6291460
  303.7 4.6 copy-start.54
  308.1 5.4 %collective-permute-start.7 = (bf16[2,160,1024]{2,1,0:T(8,128)(2,1)S(1)}, bf16[2,160,1024]{2,1,0:T(8,128)(2,1)S(1)}, u32[]{:S(2)}, u32[]{:S(2)}) collective-permute-start(bf16[2,160,1024]{2,1,0:T(8,128)(2,1)S(1)} %bitcast.246), channel_id=1, source_target_pairs={{0,1},{1,0},{2,3},{3,2},{4,5},{5,4},{6,7},{7,6},{8,9},{9,8},{10,11... | collective-permute-start | bytes 1966088 | tf_op jit(solution)/shard_map/ppermute | solution.py:26
  312.8 121.8 %collective-permute-start.12 = (bf16[2,160,1024]{2,1,0:T(8,128)(2,1)S(1)}, bf16[2,160,1024]{2,1,0:T(8,128)(2,1)}, u32[]{:S(2)}, u32[]{:S(2)}) collective-permute-start(bf16[2,160,1024]{2,1,0:T(8,128)(2,1)S(1)} %bitcast.247), channel_id=1, source_target_pairs={{0,1},{1,0},{2,3},{3,2},{4,5},{5,4},{6,7},{7,6},{8,9},{9,8},{10,11... | collective-permute-start | bytes 1966088 | tf_op jit(solution)/shard_map/ppermute | solution.py:26
  313.5 3.5 copy-start.22
  314.5 124.3 %collective-permute-start.8 = (bf16[160,1024]{1,0:T(8,128)(2,1)}, bf16[160,1024]{1,0:T(8,128)(2,1)}, u32[]{:S(2)}, u32[]{:S(2)}) collective-permute-start(bf16[160,1024]{1,0:T(8,128)(2,1)} %fusion.42), channel_id=1, source_target_pairs={{0,2},{2,0},{1,3},{3,1},{4,6},{6,4},{5,7},{7,5},{8,10},{10,8},{9,1... | collective-permute-start | bytes 983048 | tf_op jit(solution)/shard_map/ppermute | solution.py:22
  317.1 121.7 %copy-start.37 = (f32[1024]{0:T(1024)S(1)}, f32[1024]{0:T(1024)}, u32[]{:S(2)}) copy-start(f32[1024]{0:T(1024)} %get-tuple-element.88) | copy-start | bytes 12292
  433.0 7.7 %collective-permute-start.14 = (bf16[32,1024]{1,0:T(8,128)(2,1)S(1)}, bf16[32,1024]{1,0:T(8,128)(2,1)S(1)}, u32[]{:S(2)}, u32[]{:S(2)}) collective-permute-start(bf16[32,1024]{1,0:T(8,128)(2,1)S(1)} %select_bitcast_fusion), channel_id=1, source_target_pairs={{0,64},{64,0},{1,65},{65,1},{2,66},{66,2},{3,67},{67,3},{4,68},{68... | collective-permute-start | bytes 196616 | tf_op jit(solution)/shard_map/ppermute | solution.py:200
  434.6 6.0 %copy-start.19 = (f32[320,1024]{1,0:T(8,128)S(1)}, f32[320,1024]{1,0:T(8,128)}, u32[]{:S(2)}) copy-start(f32[320,1024]{1,0:T(8,128)} %get-tuple-element.102) | copy-start | bytes 3932164
  436.0 10.4 %collective-permute-start.13 = (bf16[160,1024]{1,0:T(8,128)(2,1)S(1)}, bf16[160,1024]{1,0:T(8,128)(2,1)S(1)}, u32[]{:S(2)}, u32[]{:S(2)}) collective-permute-start(bf16[160,1024]{1,0:T(8,128)(2,1)S(1)} %fusion.43), channel_id=1, source_target_pairs={{0,2},{2,0},{1,3},{3,1},{4,6},{6,4},{5,7},{7,5},{8,10},{10,8},{9,1... | collective-permute-start | bytes 983048 | tf_op jit(solution)/shard_map/ppermute | solution.py:22
  440.6 7.2 %slice-start.4 = ((f32[4,160]{1,0:T(4,128)}), f32[1,160]{1,0:T(1,128)S(1)}, s32[]{:S(2)}) async-start(f32[4,160]{1,0:T(4,128)} %copy-done.34), calls=%async_computation.8 | async-start | bytes 2048 | tf_op jit(solution)/shard_map/slice | solution.py:267
  (17 other events, 21.4 us)
Sparse Core Ops, SparseCore 0:
  104.4 47.9 all-gather.2
  303.8 127.6 all-reduce.5
